TPU v7x, 512 devices: a whole 4x4x16 slice. The times are simulated.
512 devices in a mesh: gx: 32 (over y, x, core), gy: 16 (over z).
Axes of the slice: x: 4, y: 4, z: 16, core: 2. Of those that a mesh axis runs over, the one named last changes fastest.
Arguments:
- pressure: float32 [512, 3, 8192], P('gx', None, 'gy'), may hold values from -6 to 6
- exchange_rates: float32 [512, 2, 8192], P('gx', None, 'gy'), may hold values from 0.05 to 0.45
- x_blocks: bfloat16 [512, 27, 8192], P('gx', None, 'gy')
- y_blocks: bfloat16 [512, 27, 8192], P('gx', None, 'gy')
- panels: bfloat16 [2048, 4, 512], P(('gx', 'gy')), may hold values from 0.19921875 to 2
- outlet_tiles: int32 [2048, 4], P(('gx', 'gy')), may hold values from 0 to 31, as said below
- outlet_counts: int32 [2048], P(('gx', 'gy')), may hold values from 1 to 4, as said below
- labels: int32 [512, 8192], P('gx', 'gy'), may hold values from 0 to 2047, as said below
Outputs:
- pressure_next: float32 [512, 3, 8192], P('gx', None, 'gy')
Inputs may be any that keep to these rules, and one draw needn't show every extreme that they name: `outlet_tiles`: an outlet's 4 listed tiles are distinct; its first is the gx index of the device that holds it, each other entry is that index plus a nonzero offset modulo the number of tiles along gx. `outlet_counts`: the first outlet of every device feeds all 4 of its listed tiles. `labels`: A voxel's outlet is held by a device with the voxel's gy index and feeds the voxel's tile: x // 16 is among its first outlet_counts tiles.
All inputs are finite; a program needn't handle non-finite values.
Results may differ from a plain program's by a relative error of at most 0.0013.
Values may be sent and summed in bfloat16 or wider, within the bound.
No kernel may reach another device: no remote copies, remote signals or barrier semaphores. Data moves between devices by JAX's collectives and lax.ppermute only.
A program may use at most 64 MiB of HBM per device.

v0:
```python
import jax
import jax.numpy as jnp
from jax import lax
from jax.experimental import pallas as pl
from jax.experimental.pallas import tpu as pltpu
from jax.sharding import PartitionSpec as P

F32 = jnp.float32
BF16 = jnp.bfloat16
CX, CY, NZ = 16, 32, 16
TX, TY = 32, 16
NEAR = [[4 * q + k for k in range(4)] for q in range(4)]
FAR = [[4 * q + k for q in range(4)] for k in range(4)]
ROWS = 72
LANES = 128
GROUPS = 4
MAP = 33
VMEM = pl.BlockSpec(memory_space=pltpu.VMEM)
SMEM = pl.BlockSpec(memory_space=pltpu.SMEM)
PARAMS = pltpu.CompilerParams(vmem_limit_bytes=32 * 1024 * 1024)


def mm(a, b):
    return [
        a[3 * r] * b[c] + a[3 * r + 1] * b[3 + c] + a[3 * r + 2] * b[6 + c]
        for r in range(3)
        for c in range(3)
    ]


def mv(a, v):
    return [a[3 * r] * v[0] + a[3 * r + 1] * v[1] + a[3 * r + 2] * v[2] for r in range(3)]


def add(a, b):
    return [x + y for x, y in zip(a, b)]


def iota(shape, axis):
    return lax.broadcasted_iota(jnp.int32, shape, axis)


def swap_blocks(parts):
    block = iota(parts[0].shape, 1) // NZ
    for bit in (1, 2, 4):
        low = (block & bit) == 0
        fresh = list(parts)
        for i in range(8):
            if i & bit == 0:
                first, second = parts[i], parts[i | bit]
                fresh[i] = jnp.where(low, first, pltpu.roll(second, bit * NZ, 1))
                fresh[i | bit] = jnp.where(low, pltpu.roll(first, LANES - bit * NZ, 1), second)
        parts = fresh
    return parts


def load_blocks(blocks, coef):
    for k in range(27):
        rows = blocks[k].astype(F32)
        for g in range(GROUPS):
            coef[pl.ds(g * 432 + k * CX, CX), :] = rows[:, g * LANES : (g + 1) * LANES]


def x_matrix(coef, x, first):
    return [coef[pl.ds((first + k) * CX + x, GROUPS, stride=432), :] for k in range(9)]


def depth(v, z):
    up = jnp.where(z < NZ - 1, pltpu.roll(v, LANES - 1, 1) - v, 0.0)
    down = jnp.where(z > 0, v - pltpu.roll(v, 1, 1), 0.0)
    return up - down


def prepare_x(*refs):
    inputs, (packed, base) = refs[0:7], refs[7:9]
    buffers, arrived = refs[9:16], refs[16]
    coef, fields, prefix, feats, pan = refs[17:]
    copies = [pltpu.make_async_copy(inputs[k], buffers[k], arrived.at[k]) for k in range(7)]
    for copy in copies:
        copy.start()
    pressure, exchange, blocks, labels, panels, tiles, counts = buffers
    copies[0].wait()
    copies[1].wait()
    for g in range(GROUPS):
        cut = slice(g * LANES, (g + 1) * LANES)
        for k in range(3):
            fields[pl.ds(g * 128 + k * CX, CX), :] = pressure[k, :, cut]
        for x in range(CX):
            fields[pl.ds(g * 128 + 64 + x * 2, 2), :] = exchange[x, :, cut]
    z = iota((GROUPS, LANES), 1) & (NZ - 1)
    for x in range(CX):
        field = [fields[pl.ds(k * CX + x, GROUPS, stride=128), :] for k in range(3)]
        rates = [fields[pl.ds(64 + x * 2 + k, GROUPS, stride=128), :] for k in range(2)]
        inflow = rates[0] * (field[0] - field[1])
        outflow = rates[1] * (field[1] - field[2])
        base[x * 3] = field[0] - inflow + 0.2 * depth(field[0], z)
        base[x * 3 + 1] = field[1] + inflow - outflow + 0.2 * depth(field[1], z)
        base[x * 3 + 2] = field[2] + outflow + 0.2 * depth(field[2], z)
    for g in range(GROUPS):
        feats[pl.ds(g * 256 + 96, 160), :] = jnp.zeros((160, LANES), F32)
    copies[2].wait()
    load_blocks(blocks, coef)
    copies[3].wait()
    where_from = labels[...]
    where_from = (where_from // (TY * 4)) * 4 + (where_from & 3)
    where_from = where_from.astype(F32)
    for g in range(GROUPS):
        feats[pl.ds(g * 256 + 96, CX), :] = where_from[:, g * LANES : (g + 1) * LANES]

    u = x_matrix(coef, 0, 18)
    for x in range(1, CX):
        for k in range(9):
            prefix[x * 9 + k] = u[k]
        if x < CX - 1:
            u = mm(u, x_matrix(coef, x, 18))
    c_map = mm(u, x_matrix(coef, CX - 1, 18))

    def put(row, value):
        feats[pl.ds(row, GROUPS, stride=256), :] = value

    s, w = None, None
    b, e = None, None
    for x in reversed(range(CX)):
        ux = [prefix[x * 9 + k] for k in range(9)] if x > 0 else None
        if x == CX - 1:
            w = ux
        else:
            p = x_matrix(coef, x + 1, 0)
            s = p if s is None else mm(s, p)
            w = mm(w, p)
            if x > 0:
                w = add(w, ux)
            else:
                for k in (0, 4, 8):
                    w[k] = w[k] + 1.0
        gain = x_matrix(coef, x, 9)
        r = [base[x * 3 + k] for k in range(3)]
        column = [gain[0], gain[3], gain[6]]
        pushed = mv(gain, r)
        kb = column if s is None else mv(s, column)
        ke = mv(w, column)
        sb = pushed if s is None else mv(s, pushed)
        se = mv(w, pushed)
        b = sb if b is None else add(b, sb)
        e = se if e is None else add(e, se)
        for k in range(3):
            put(k * CX + x, kb[k])
            put((3 + k) * CX + x, ke[k])
    p = x_matrix(coef, 0, 0)
    values = mm(s, p) + c_map + mm(w, p) + b + e
    for k in range(MAP):
        high = values[k].astype(BF16).astype(F32)
        put(128 + k, high)
        put(128 + MAP + k, values[k] - high)

    for k in range(4, 7):
        copies[k].wait()
    for k in range(4):
        pan[pl.ds(k * 4, 4), :] = panels[k].astype(F32)
    row, column = iota((16, 4), 0), iota((16, 4), 1)
    listed = jnp.concatenate([jnp.broadcast_to(tiles[k : k + 1, :], (4, 4)) for k in range(4)], axis=0)
    limits = jnp.broadcast_to(counts[...], (16, 4))
    listed = jnp.sum(jnp.where(column == (row & 3), listed.astype(F32), 0.0), axis=1, keepdims=True)
    limits = jnp.sum(jnp.where(column == row // 4, limits.astype(F32), 0.0), axis=1, keepdims=True)
    routes = jnp.where((row[:, 0:1] & 3).astype(F32) < limits, listed, -1.0)
    routes = jnp.broadcast_to(routes, (16, LANES))
    routes = jnp.concatenate([routes] * 8, axis=0)
    lane = iota((LANES, LANES), 1)
    for g in range(GROUPS):
        rows = slice(g * LANES, (g + 1) * LANES)
        slab = pan[:, g * LANES : (g + 1) * LANES]
        pieces = [pltpu.roll(slab, (112 - i * NZ) % LANES, 1) if i < 7 else slab for i in range(8)]
        first = feats[pl.ds(g * 256, LANES), :].T
        first = jnp.where(lane >= 112, jnp.concatenate(pieces, axis=0), first)
        packed[rows, 0:LANES] = first.astype(BF16)
        second = feats[pl.ds(g * 256 + LANES, LANES), :].T
        second = jnp.where(lane == 72, routes, second)
        packed[rows, LANES : 2 * LANES] = second.astype(BF16)


def solve_x(received, answer, low, high, spread, target, out):
    for g in range(GROUPS):
        rows = slice(g * LANES, (g + 1) * LANES)
        low[rows, :] = received[rows, 0:LANES].astype(F32).T
        high[rows, :] = received[rows, LANES : 2 * LANES].astype(F32).T
    r_id, c_id = iota((LANES, LANES), 0), iota((LANES, LANES), 1)
    lane = iota((512, LANES), 1)
    copy_panel = ((r_id >= 112) & ((r_id - 112) == (c_id & (NZ - 1)))).astype(F32).astype(BF16)
    copy_route = (r_id == 72).astype(F32).astype(BF16)
    panel_part = received[:, 0:LANES].astype(F32)
    panel_part = jnp.where(lane >= 112, panel_part, 0.0).astype(BF16)
    route_part = received[:, LANES : 2 * LANES].astype(F32)
    route_part = jnp.where(lane == 72, route_part, 0.0).astype(BF16)
    spread[...] = jnp.dot(panel_part, copy_panel, preferred_element_type=F32)
    target[...] = jnp.dot(route_part, copy_route, preferred_element_type=F32)
    tile_lane = (c_id // NZ).astype(F32)
    for g in range(GROUPS):
        table = None
        for j in range(4):
            hit = target[pl.ds(j, LANES, stride=4), :] == tile_lane + 8.0 * g
            part = jnp.where(hit, spread[pl.ds(j, LANES, stride=4), :], 0.0)
            table = part if table is None else table + part
        position = low[pl.ds(g * LANES + 96, CX), :].astype(jnp.int32)
        found = []
        for half in range(2):
            place = position[half * 8 : half * 8 + 8, :]
            inner, outer = place & 7, place // 8
            picked = jnp.zeros((8, LANES), F32)
            for o in range(16):
                chosen = jnp.take_along_axis(table[o * 8 : o * 8 + 8, :], inner, axis=0)
                picked = jnp.where(outer == o, chosen, picked)
            found.append(picked)
        source = jnp.concatenate(found, axis=0)
        out[pl.ds(g * LANES + 24, CX), :] = source
        for k in range(6):
            response = low[pl.ds(g * LANES + k * CX, CX), :]
            extra = jnp.sum(response * source, axis=0, keepdims=True)
            at = pl.ds(g * LANES + 27 + k, 1)
            high[at, :] = high[at, :] + extra

    def value(k):
        return high[pl.ds(k, 8, stride=LANES), :] + high[pl.ds(MAP + k, 8, stride=LANES), :]

    lanes8 = iota((8, LANES), 1)
    tile = iota((8, LANES), 0) * 8 + lanes8 // NZ

    def before(v, d, fill):
        if d < 8:
            turned = pltpu.roll(v, d * NZ, 1)
            moved = jnp.where(lanes8 >= d * NZ, turned, pltpu.roll(turned, 1, 0))
        else:
            moved = pltpu.roll(v, d // 8, 0)
        return jnp.where(tile >= d, moved, fill)

    def after(v, d, fill):
        if d < 8:
            turned = pltpu.roll(v, LANES - d * NZ, 1)
            moved = jnp.where(lanes8 < LANES - d * NZ, turned, pltpu.roll(turned, 7, 0))
        else:
            moved = pltpu.roll(v, 8 - d // 8, 0)
        return jnp.where(tile + d < TX, moved, fill)

    def scan(matrix, vector, shift):
        for d in (1, 2, 4, 8, 16):
            vector_now = add(mv(matrix, [shift(v, d, 0.0) for v in vector]), vector)
            if d < 16:
                matrix = mm(matrix, [shift(m, d, 1.0 if k in (0, 4, 8) else 0.0) for k, m in enumerate(matrix)])
            vector = vector_now
        return [shift(v, 1, 0.0) for v in vector]

    enter = scan([value(k) for k in range(9)], [value(27 + k) for k in range(3)], before)
    pushed = add(mv([value(18 + k) for k in range(9)], enter), [value(30 + k) for k in range(3)])
    finish = scan([value(9 + k) for k in range(9)], pushed, after)
    for k, v in enumerate(enter + finish):
        for piece in range(3):
            part = v.astype(BF16).astype(F32)
            out[pl.ds(piece * 6 + k, 8, stride=LANES), :] = part
            v = v - part
    for g in range(GROUPS):
        rows = slice(g * LANES, (g + 1) * LANES)
        answer[rows, :] = out[rows, :].T.astype(BF16)


def prepare_y(blocks, turned, parts, whole, plain, coef):
    load_blocks(blocks, plain)
    for half in range(2):
        for g in range(GROUPS):
            rows = swap_blocks([plain[pl.ds(g * 432 + half * 8 + i, 27, stride=CX), :] for i in range(8)])
            for y in range(8):
                coef[pl.ds((g * 2 + half) * 256 + y * 32, 27), :] = rows[y]
    phi, u, d_map = None, None, None
    for y in range(8):
        block = [coef[pl.ds(y * 32 + k, 8, stride=256), :] for k in range(27)]
        for k in range(27):
            turned[y * 27 + k] = block[k]
        phi = block[0:9] if y == 0 else mm(block[0:9], phi)
        d_map = phi if y == 0 else add(d_map, mm(u, phi))
        u = block[18:27] if y == 0 else mm(u, block[18:27])
    for k, v in enumerate(phi + u + d_map):
        parts[pl.ds(k * 8, 8), :] = v
    a, c, d = [quarter(parts, 0, 9 * k, 9) for k in range(3)]
    for l in range(1, GROUPS):
        a_l, c_l, d_l = [quarter(parts, l, 9 * k, 9) for k in range(3)]
        d = add(mm(mm(c, d_l), a), d)
        a = mm(a_l, a)
        c = mm(c, c_l)
    for k, v in enumerate(a + c + d):
        whole[pl.ds(k * 2, 2), :] = v
    whole[pl.ds(54, 2), :] = jnp.zeros((2, LANES), F32)


def quarter(ref, l, first, count):
    return [ref[pl.ds((first + k) * 8 + l * 2, 2), :] for k in range(count)]


def finish_x(received, base, blocks, turned, parts, whole, sent, values, ends, coef, low, stage, lined):
    load_blocks(blocks, coef)
    for g in range(GROUPS):
        rows = slice(g * LANES, (g + 1) * LANES)
        low[rows, :] = received[rows, :].astype(F32).T

    def entry(k):
        rows = [low[pl.ds(piece * 6 + k, GROUPS, stride=LANES), :] for piece in range(3)]
        return rows[0] + rows[1] + rows[2]

    f = [entry(k) for k in range(3)]
    a = [entry(3 + k) for k in range(3)]
    forward = []
    for x in range(CX):
        source = low[pl.ds(24 + x, GROUPS, stride=LANES), :]
        r = [base[x * 3] + source, base[x * 3 + 1], base[x * 3 + 2]]
        f = add(mv(x_matrix(coef, x, 0), f), mv(x_matrix(coef, x, 9), r))
        forward.append(f)
    for x in reversed(range(CX)):
        a = add(mv(x_matrix(coef, x, 18), a), forward[x])
        for k in range(3):
            stage[pl.ds(x * 16 + k * 4, 4), :] = a[k]
    for half in range(2):
        rows = swap_blocks([stage[pl.ds((half * 8 + i) * 16, 16), :] for i in range(8)])
        for y in range(8):
            for k in range(3):
                lined[pl.ds(half * 24 + y * 3 + k, 4, stride=48), :] = rows[y][k * 4 : k * 4 + 4, :]
    f, forward = None, []
    for y in range(8):
        r = [lined[pl.ds(y * 3 + k, 8, stride=24), :] for k in range(3)]
        pushed = mv([turned[y * 27 + 9 + k] for k in range(9)], r)
        for k in range(3):
            values[y * 3 + k] = pushed[k]
        f = pushed if f is None else add(mv([turned[y * 27 + k] for k in range(9)], f), pushed)
        forward.append(f)
    a = None
    for y in reversed(range(8)):
        a = forward[y] if a is None else add(mv([turned[y * 27 + 18 + k] for k in range(9)], a), forward[y])
    for k, v in enumerate(forward[7] + a):
        ends[pl.ds(k * 8, 8), :] = v
    enter, f = [], None
    for l in range(GROUPS):
        enter.append(f)
        b_l = quarter(ends, l, 0, 3)
        f = b_l if f is None else add(mv(quarter(parts, l, 0, 9), f), b_l)
    a = None
    for l in reversed(range(GROUPS)):
        now = quarter(ends, l, 3, 3)
        if enter[l] is not None:
            now = add(now, mv(quarter(parts, l, 18, 9), enter[l]))
        a = now if a is None else add(mv(quarter(parts, l, 9, 9), a), now)
    put_map(sent, [whole[pl.ds(k * 2, 2), :] for k in range(27)] + f + a)


def put_map(sent, values):
    for k, v in enumerate(values):
        sent[pl.ds(k * 2, 2), :] = v
    sent[pl.ds(66, 6), :] = jnp.zeros((6, LANES), F32)
    for i in range(1, 4):
        sent[pl.ds(i * ROWS, ROWS), :] = sent[pl.ds(0, ROWS), :]


def get_map(ref, i):
    v = [ref[pl.ds(i * ROWS + k * 2, 2), :] for k in range(MAP)]
    return v[0:9], v[9:18], v[18:27], v[27:30], v[30:33]


def join_y(received, sent):
    a, c, d, b, e = get_map(received, 0)
    for i in range(1, 4):
        a1, c1, d1, b1, e1 = get_map(received, i)
        e = add(mv(c, add(mv(d1, b), e1)), e)
        d = add(mm(c, mm(d1, a)), d)
        b = add(mv(a1, b), b1)
        a = mm(a1, a)
        c = mm(c, c1)
    put_map(sent, a + c + d + b + e)


def narrow(received, mine, enter, finish):
    maps = [get_map(received, i) for i in range(4)]
    fs = [enter]
    for i in range(3):
        fs.append(add(mv(maps[i][0], fs[i]), maps[i][3]))
    ends = [None, None, None, finish]
    for i in (3, 2, 1):
        _, c, d, _, e = maps[i]
        ends[i - 1] = add(add(mv(c, ends[i]), mv(d, fs[i])), e)
    enter, finish = fs[0], ends[0]
    for i in range(1, 4):
        enter = [jnp.where(mine == i, n, o) for n, o in zip(fs[i], enter)]
        finish = [jnp.where(mine == i, n, o) for n, o in zip(ends[i], finish)]
    return enter, finish


def finish_y(place, near, far, values, ends, turned, parts, result, edge):
    me = place[0]
    zero = [jnp.zeros((2, LANES), F32) for _ in range(3)]
    enter, finish = narrow(far, me // 4, zero, zero)
    enter, finish = narrow(near, me % 4, enter, finish)
    f = enter
    inside = []
    for l in range(GROUPS):
        inside.append(f)
        for k in range(3):
            edge[pl.ds(k * 8 + l * 2, 2), :] = f[k]
        if l < GROUPS - 1:
            f = add(mv(quarter(parts, l, 0, 9), f), quarter(ends, l, 0, 3))
    a = finish
    for l in reversed(range(GROUPS)):
        for k in range(3):
            edge[pl.ds(24 + k * 8 + l * 2, 2), :] = a[k]
        if l > 0:
            a = add(
                add(mv(quarter(parts, l, 9, 9), a), mv(quarter(parts, l, 18, 9), inside[l])),
                quarter(ends, l, 3, 3),
            )
    f = [edge[pl.ds(k * 8, 8), :] for k in range(3)]
    a = [edge[pl.ds(24 + k * 8, 8), :] for k in range(3)]
    forward = []
    for y in range(8):
        f = add(mv([turned[y * 27 + k] for k in range(9)], f), [values[y * 3 + k] for k in range(3)])
        forward.append(f)
    solved = [None] * 8
    for y in reversed(range(8)):
        a = add(mv([turned[y * 27 + 18 + k] for k in range(9)], a), forward[y])
        solved[y] = a
    for k in range(3):
        rows = swap_blocks([solved[y][k] for y in range(8)])
        for x in range(8):
            for g in range(GROUPS):
                for half in range(2):
                    at = g * 2 + half
                    result[k, pl.ds(half * 8 + x, 1), g * LANES : (g + 1) * LANES] = rows[x][at : at + 1, :]


def body(pressure, exchange_rates, x_blocks, y_blocks, panels, outlet_tiles, outlet_counts, labels):
    shape = jax.ShapeDtypeStruct
    pressure, x_blocks, y_blocks = [jnp.transpose(v, (1, 0, 2)) for v in (pressure, x_blocks, y_blocks)]
    inputs = (pressure, exchange_rates, x_blocks, labels, panels, outlet_tiles, outlet_counts.reshape(1, 4))
    packed, base = pl.pallas_call(
        prepare_x,
        out_shape=(shape((512, 256), BF16), shape((CX * 3, GROUPS, LANES), F32)),
        in_specs=[pl.BlockSpec(memory_space=pltpu.HBM)] * 7,
        out_specs=(VMEM, VMEM),
        scratch_shapes=[pltpu.VMEM(v.shape, v.dtype) for v in inputs]
        + [
            pltpu.SemaphoreType.DMA((7,)),
            pltpu.VMEM((1728, LANES), F32),
            pltpu.VMEM((512, LANES), F32),
            pltpu.VMEM((CX * 9, GROUPS, LANES), F32),
            pltpu.VMEM((1024, LANES), F32),
            pltpu.VMEM((16, 512), F32),
        ],
        name="prepare_x",
    )(*inputs)
    received = lax.all_to_all(packed, "gx", split_axis=0, concat_axis=0, tiled=True)
    turned, parts, whole = pl.pallas_call(
        prepare_y,
        out_shape=(
            shape((8 * 27, 8, LANES), F32),
            shape((27 * 8, LANES), F32),
            shape((56, LANES), F32),
        ),
        in_specs=[VMEM],
        out_specs=(VMEM,) * 3,
        scratch_shapes=[pltpu.VMEM((1728, LANES), F32), pltpu.VMEM((2048, LANES), F32)],
        compiler_params=PARAMS,
        name="prepare_y",
    )(y_blocks)
    answer = pl.pallas_call(
        solve_x,
        out_shape=shape((512, LANES), BF16),
        in_specs=[VMEM],
        out_specs=VMEM,
        scratch_shapes=[
            pltpu.VMEM((512, LANES), F32),
            pltpu.VMEM((1024, LANES), F32),
            pltpu.VMEM((512, LANES), F32),
            pltpu.VMEM((512, LANES), F32),
            pltpu.VMEM((1024, LANES), F32),
        ],
        compiler_params=PARAMS,
        name="solve_x",
    )(received)
    entries = lax.all_to_all(answer, "gx", split_axis=0, concat_axis=0, tiled=True)
    sent, values, ends = pl.pallas_call(
        finish_x,
        out_shape=(
            shape((4 * ROWS, LANES), F32),
            shape((24, 8, LANES), F32),
            shape((48, LANES), F32),
        ),
        in_specs=[VMEM] * 6,
        out_specs=(VMEM,) * 3,
        scratch_shapes=[
            pltpu.VMEM((1728, LANES), F32),
            pltpu.VMEM((512, LANES), F32),
            pltpu.VMEM((256, LANES), F32),
            pltpu.VMEM((192, LANES), F32),
        ],
        compiler_params=PARAMS,
        name="finish_x",
    )(entries, base, x_blocks, turned, parts, whole)
    near = lax.all_to_all(sent, "gy", split_axis=0, concat_axis=0, tiled=True, axis_index_groups=NEAR)
    joined = pl.pallas_call(
        join_y,
        out_shape=shape((4 * ROWS, LANES), F32),
        in_specs=[VMEM],
        out_specs=VMEM,
        compiler_params=PARAMS,
        name="join_y",
    )(near)
    far = lax.all_to_all(joined, "gy", split_axis=0, concat_axis=0, tiled=True, axis_index_groups=FAR)
    place = lax.axis_index("gy").astype(jnp.int32).reshape(1)
    result = pl.pallas_call(
        finish_y,
        out_shape=shape((3, CX, 512), F32),
        in_specs=[SMEM] + [VMEM] * 6,
        out_specs=VMEM,
        scratch_shapes=[pltpu.VMEM((48, LANES), F32)],
        compiler_params=PARAMS,
        name="finish_y",
    )(place, near, far, values, ends, turned, parts)
    return jnp.transpose(result, (1, 0, 2))


def solution(mesh):
    in_specs = (
        P("gx", None, "gy"),
        P("gx", None, "gy"),
        P("gx", None, "gy"),
        P("gx", None, "gy"),
        P(("gx", "gy"), None, None),
        P(("gx", "gy"), None),
        P(("gx", "gy")),
        P("gx", "gy"),
    )
    out_specs = P("gx", None, "gy")
    return jax.shard_map(body, mesh=mesh, in_specs=in_specs, out_specs=out_specs, check_vma=False)
```

profile of v0, /device:TPU:2, one launch (start us, length us, event | category | flops | bytes accessed | tf_op | source)
XLA Modules:
  0.0 74.7 jit_solution(16743253346457982268)
XLA Ops:
  0.0 2.8 %prepare_x.1 = (bf16[512,256]{1,0:T(8,128)(2,1)}, f32[48,4,128]{2,1,0:T(4,128)}) custom-call(f32[3,16,512]{2,1,0:T(8,128)} %bitcast.24, f32[16,2,512]{2,1,0:T(2,128)} %refs_1_.1, bf16[27,16,512]{2,1,0:T(8,128)(2,1)} %bitcast.14, s32[16,512]{1,0:T(8,128)} %refs_3_.1, bf16[4,4,512]{2,1,0:T(4,128)(2,1)} %refs_4_.1, s32[4,4]{1,0:T(4,128)} %refs_5_.1, ...), custom_call_target="tpu_custom_call" | custom-call | tf_op jit(solution)/shard_map/prepare_x/pallas_call | solution.py:436
  2.8 17.2 %all_to_all.44 = bf16[32,16,256]{2,1,0:T(8,128)(2,1)S(1)} all-to-all(bf16[32,16,256]{2,1,0:T(8,128)(2,1)} %bitcast.23), channel_id=1, replica_groups=mesh['gx'=32,'gy'=16] {'gx'}, dimensions={0} | all-to-all | bytes 524288 | tf_op jit(solution)/shard_map/all_to_all | solution.py:452
  20.1 0.0 copy-start.1
  20.1 1.8 %solve_x.1 = bf16[512,128]{1,0:T(8,128)(2,1)} custom-call(bf16[512,256]{1,0:T(8,128)(2,1)S(1)} %bitcast.18), custom_call_target="tpu_custom_call" | custom-call | tf_op jit(solution)/shard_map/solve_x/pallas_call | solution.py:466
  21.9 0.0 copy-start
  21.9 5.1 %all-to-all-start.1 = ((bf16[32,16,128]{2,1,0:T(8,128)(2,1)}), bf16[32,16,128]{2,1,0:T(8,128)(2,1)S(1)}, u32[]{:S(2)}, u32[]{:S(2)}) async-start(bf16[32,16,128]{2,1,0:T(8,128)(2,1)} %bitcast.6), calls=%async_computation.1 | async-start | bytes 262144 | tf_op jit(solution)/shard_map/all_to_all | solution.py:481
  27.0 0.0 copy-done.1
  27.0 0.0 copy-start.2
  27.0 2.1 %prepare_y.1 = (f32[216,8,128]{2,1,0:T(8,128)S(1)}, f32[216,128]{1,0:T(8,128)S(1)}, f32[56,128]{1,0:T(8,128)S(1)}) custom-call(bf16[27,16,512]{2,1,0:T(8,128)(2,1)S(1)} %bitcast.21), custom_call_target="tpu_custom_call" | custom-call | tf_op jit(solution)/shard_map/prepare_y/pallas_call | solution.py:453
  29.1 4.6 %all-to-all-done.1 = bf16[32,16,128]{2,1,0:T(8,128)(2,1)S(1)} async-done(((bf16[32,16,128]{2,1,0:T(8,128)(2,1)}), bf16[32,16,128]{2,1,0:T(8,128)(2,1)S(1)}, u32[]{:S(2)}, u32[]{:S(2)}) %all-to-all-start.1) | async-done | bytes 131104 | tf_op jit(solution)/shard_map/all_to_all | solution.py:481
  33.7 0.0 copy-done
  33.7 0.0 copy-done.2
  33.7 0.8 %finish_x.1 = (f32[288,128]{1,0:T(8,128)S(1)}, f32[24,8,128]{2,1,0:T(8,128)S(1)}, f32[48,128]{1,0:T(8,128)S(1)}) custom-call(bf16[512,128]{1,0:T(8,128)(2,1)S(1)} %bitcast.20, f32[48,4,128]{2,1,0:T(4,128)S(1)} %copy-done.2, bf16[27,16,512]{2,1,0:T(8,128)(2,1)S(1)} %bitcast.15, f32[216,8,128]{2,1,0:T(8,128)S(1)} %get-tuple-element.15.turned, ...), custom_call_target="tpu_custom_call" | custom-call | tf_op jit(solution)/shard_map/finish_x/pallas_call | solution.py:482
  34.5 10.6 %all_to_all.45 = f32[4,72,128]{2,1,0:T(8,128)S(1)} all-to-all(f32[4,72,128]{2,1,0:T(8,128)S(1)} %bitcast.22), channel_id=1, replica_groups={{0,1,2,3},{4,5,6,7},{8,9,10,11},{12,13,14,15},{16,17,18,19},{20,21,22,2..., dimensions={0} | all-to-all | bytes 294912 | tf_op jit(solution)/shard_map/all_to_all | solution.py:500
  45.1 0.8 %join_y.1 = f32[288,128]{1,0:T(8,128)} custom-call(f32[288,128]{1,0:T(8,128)S(1)} %bitcast.16), custom_call_target="tpu_custom_call" | custom-call | tf_op jit(solution)/shard_map/join_y/pallas_call | solution.py:501
  45.9 12.4 %all-to-all-start.3 = ((f32[4,72,128]{2,1,0:T(8,128)}), f32[4,72,128]{2,1,0:T(8,128)S(1)}, u32[]{:S(2)}, u32[]{:S(2)}) async-start(f32[4,72,128]{2,1,0:T(8,128)} %bitcast.11), calls=%async_computation.3 | async-start | bytes 294912 | tf_op jit(solution)/shard_map/all_to_all | solution.py:509
  58.2 15.4 %all-to-all-done.3 = f32[4,72,128]{2,1,0:T(8,128)S(1)} async-done(((f32[4,72,128]{2,1,0:T(8,128)}), f32[4,72,128]{2,1,0:T(8,128)S(1)}, u32[]{:S(2)}, u32[]{:S(2)}) %all-to-all-start.3) | async-done | bytes 147488 | tf_op jit(solution)/shard_map/all_to_all | solution.py:509
  73.6 1.0 %finish_y.1 = f32[3,16,512]{2,1,0:T(8,128)} custom-call(s32[1]{0:T(128)} %bitcast.place, f32[288,128]{1,0:T(8,128)S(1)} %bitcast.17, f32[288,128]{1,0:T(8,128)S(1)} %bitcast.19, f32[24,8,128]{2,1,0:T(8,128)S(1)} %get-tuple-element.19.values, f32[48,128]{1,0:T(8,128)S(1)} %get-tuple-element.20.ends, f32[216,8,128]{2,1,0:T(8,128)S(1)} %get-tuple-element.15.turned, ...), custom_call_target="tpu_custom_call" | custom-call | tf_op jit(solution)/shard_map/finish_y/pallas_call | solution.py:511
Async XLA Ops:
  20.1 7.0 %copy-start.1 = (bf16[16,27,512]{2,0,1:T(8,128)(2,1)S(1)}, bf16[16,27,512]{2,0,1:T(8,128)(2,1)}, u32[]{:S(2)}) copy-start(bf16[16,27,512]{2,0,1:T(8,128)(2,1)} %param.11) | copy-start | bytes 1327108
  21.9 11.8 %copy-start = (bf16[16,27,512]{2,0,1:T(8,128)(2,1)S(1)}, bf16[16,27,512]{2,0,1:T(8,128)(2,1)}, u32[]{:S(2)}) copy-start(bf16[16,27,512]{2,0,1:T(8,128)(2,1)} %param.10) | copy-start | bytes 1327108
  21.9 11.8 %all-to-all-start.1 = ((bf16[32,16,128]{2,1,0:T(8,128)(2,1)}), bf16[32,16,128]{2,1,0:T(8,128)(2,1)S(1)}, u32[]{:S(2)}, u32[]{:S(2)}) async-start(bf16[32,16,128]{2,1,0:T(8,128)(2,1)} %bitcast.6), calls=%async_computation.1 | async-start | bytes 262144 | tf_op jit(solution)/shard_map/all_to_all | solution.py:481
  27.0 6.7 %copy-start.2 = (f32[48,4,128]{2,1,0:T(4,128)S(1)}, f32[48,4,128]{2,1,0:T(4,128)}, u32[]{:S(2)}) copy-start(f32[48,4,128]{2,1,0:T(4,128)} %get-tuple-element.14.base) | copy-start | bytes 294916
  45.9 27.8 %all-to-all-start.3 = ((f32[4,72,128]{2,1,0:T(8,128)}), f32[4,72,128]{2,1,0:T(8,128)S(1)}, u32[]{:S(2)}, u32[]{:S(2)}) async-start(f32[4,72,128]{2,1,0:T(8,128)} %bitcast.11), calls=%async_computation.3 | async-start | bytes 294912 | tf_op jit(solution)/shard_map/all_to_all | solution.py:509
where the time goes:
time: 75.1 us; the launch traced here: 74.7 us
  blocking collectives  27.8 us (37%)
  waiting for transfers between devices  20 us (27%)
  starting transfers between devices  17.5 us (23%)
  Pallas kernels  9.34 us (12%)
    all_to_all x1, blocking collectives, body(): lax.all_to_all(packed, 'gx', split_axis=0, concat_axis=0, tiled=True)  17.2 us
    all_to_all x1, waiting for transfers between devices, body(): lax.all_to_all(joined, 'gy', split_axis=0, concat_axis=0, tiled=True, axi...  15.4 us
    all_to_all x1, starting transfers between devices, body(): lax.all_to_all(joined, 'gy', split_axis=0, concat_axis=0, tiled=True, axi...  12.4 us
    all_to_all x1, blocking collectives, body(): lax.all_to_all(sent, 'gy', split_axis=0, concat_axis=0, tiled=True, axis_...  10.6 us
    all_to_all x1, starting transfers between devices, body(): lax.all_to_all(answer, 'gx', split_axis=0, concat_axis=0, tiled=True)  5.1 us
    all_to_all x1, waiting for transfers between devices, body(): lax.all_to_all(answer, 'gx', split_axis=0, concat_axis=0, tiled=True)  4.58 us
    pallas_call x1, Pallas kernels, body(): pl.pallas_call(prepare_x, out_shape=(shape((512, 256), BF16), shape((CX *...  2.83 us
    pallas_call x1, Pallas kernels, body(): pl.pallas_call(prepare_y, out_shape=(shape((8 * 27, 8, LANES), F32), shap...  2.09 us
  transfers between devices with their start and end apart: 2, of which 2 were waited for; matrix products, arithmetic and copies ran while one was open for 0% of the time, Pallas kernels for 3%

commit v1 on v0

--- a/solution.py
+++ b/solution.py
@@ -261,7 +261,8 @@
         answer[rows, :] = out[rows, :].T.astype(BF16)
 
 
-def prepare_y(blocks, turned, parts, whole, plain, coef):
+def prepare_y(place, blocks, turned, parts, whole, spot, plain, coef):
+    spot[...] = jnp.full((8, LANES), place[0], jnp.int32)
     load_blocks(blocks, plain)
     for half in range(2):
         for g in range(GROUPS):
@@ -388,8 +389,8 @@
     return enter, finish
 
 
-def finish_y(place, near, far, values, ends, turned, parts, result, edge):
-    me = place[0]
+def finish_y(spot, near, far, values, ends, turned, parts, result, edge):
+    me = spot[0:2, :]
     zero = [jnp.zeros((2, LANES), F32) for _ in range(3)]
     enter, finish = narrow(far, me // 4, zero, zero)
     enter, finish = narrow(near, me % 4, enter, finish)
@@ -433,11 +434,12 @@
     shape = jax.ShapeDtypeStruct
     pressure, x_blocks, y_blocks = [jnp.transpose(v, (1, 0, 2)) for v in (pressure, x_blocks, y_blocks)]
     inputs = (pressure, exchange_rates, x_blocks, labels, panels, outlet_tiles, outlet_counts.reshape(1, 4))
+    place = lax.axis_index("gy").astype(jnp.int32).reshape(1)
     packed, base = pl.pallas_call(
         prepare_x,
         out_shape=(shape((512, 256), BF16), shape((CX * 3, GROUPS, LANES), F32)),
         in_specs=[pl.BlockSpec(memory_space=pltpu.HBM)] * 7,
-        out_specs=(VMEM, VMEM),
+        out_specs=(VMEM,) * 2,
         scratch_shapes=[pltpu.VMEM(v.shape, v.dtype) for v in inputs]
         + [
             pltpu.SemaphoreType.DMA((7,)),
@@ -450,19 +452,21 @@
         name="prepare_x",
     )(*inputs)
     received = lax.all_to_all(packed, "gx", split_axis=0, concat_axis=0, tiled=True)
-    turned, parts, whole = pl.pallas_call(
+    turned, parts, whole, spot = pl.pallas_call(
         prepare_y,
         out_shape=(
             shape((8 * 27, 8, LANES), F32),
             shape((27 * 8, LANES), F32),
             shape((56, LANES), F32),
+            shape((8, LANES), jnp.int32),
         ),
-        in_specs=[VMEM],
-        out_specs=(VMEM,) * 3,
+        in_specs=[SMEM, VMEM],
+        out_specs=(VMEM,) * 4,
         scratch_shapes=[pltpu.VMEM((1728, LANES), F32), pltpu.VMEM((2048, LANES), F32)],
         compiler_params=PARAMS,
         name="prepare_y",
-    )(y_blocks)
+    )(place, y_blocks)
+    received, whole = lax.optimization_barrier((received, whole))
     answer = pl.pallas_call(
         solve_x,
         out_shape=shape((512, LANES), BF16),
@@ -507,16 +511,15 @@
         name="join_y",
     )(near)
     far = lax.all_to_all(joined, "gy", split_axis=0, concat_axis=0, tiled=True, axis_index_groups=FAR)
-    place = lax.axis_index("gy").astype(jnp.int32).reshape(1)
     result = pl.pallas_call(
         finish_y,
         out_shape=shape((3, CX, 512), F32),
-        in_specs=[SMEM] + [VMEM] * 6,
+        in_specs=[VMEM] * 7,
         out_specs=VMEM,
         scratch_shapes=[pltpu.VMEM((48, LANES), F32)],
         compiler_params=PARAMS,
         name="finish_y",
-    )(place, near, far, values, ends, turned, parts)
+    )(spot, near, far, values, ends, turned, parts)
     return jnp.transpose(result, (1, 0, 2))
 
 

time: 75.1 us -> 73.3 us (0.976)
  blocking collectives: 27.8 us -> 49.7 us
  waiting for transfers between devices: 20 us -> 5.67 us
  starting transfers between devices: 17.5 us -> 9.45 us
  Pallas kernels: 9.34 us -> 8.1 us
    all_to_all x1 -> x2, blocking collectives: 17.2 us -> 39.1 us  [the longest x1 27.6 us: body(): lax.all_to_all(joined, 'gy', split_axis=0, concat_axis=0, tiled=True, axi...]
    all_to_all x2 -> x1, waiting for transfers between devices: 20 us -> 5.67 us  [body(): lax.all_to_all(packed, 'gx', split_axis=0, concat_axis=0, tiled=True)]
    all_to_all x2 -> x1, starting transfers between devices: 17.5 us -> 9.45 us  [body(): lax.all_to_all(packed, 'gx', split_axis=0, concat_axis=0, tiled=True)]
  transfers between devices with their start and end apart: 2 -> 1, of which waited for: 2 -> 1; matrix products, arithmetic and copies ran while one was open for 0% -> 0% of each run, Pallas kernels for 3% -> 3%
where the time goes in v1:
time: 73.3 us; the launch traced here: 73 us
  blocking collectives  49.7 us (68%)
  starting transfers between devices  9.45 us (13%)
  Pallas kernels  8.1 us (11%)
  waiting for transfers between devices  5.67 us (8%)
    all_to_all x1, blocking collectives, body(): lax.all_to_all(joined, 'gy', split_axis=0, concat_axis=0, tiled=True, axi...  27.6 us
    all_to_all x1, blocking collectives, body(): lax.all_to_all(answer, 'gx', split_axis=0, concat_axis=0, tiled=True)  11.5 us
    all_to_all x1, blocking collectives, body(): lax.all_to_all(sent, 'gy', split_axis=0, concat_axis=0, tiled=True, axis_...  10.6 us
    all_to_all x1, starting transfers between devices, body(): lax.all_to_all(packed, 'gx', split_axis=0, concat_axis=0, tiled=True)  9.45 us
    all_to_all x1, waiting for transfers between devices, body(): lax.all_to_all(packed, 'gx', split_axis=0, concat_axis=0, tiled=True)  5.67 us
    pallas_call x1, Pallas kernels, body(): pl.pallas_call(prepare_x, out_shape=(shape((512, 256), BF16), shape((CX *...  2.88 us
    pallas_call x1, Pallas kernels, body(): pl.pallas_call(prepare_y, out_shape=(shape((8 * 27, 8, LANES), F32), shap...  2.09 us
  transfers between devices with their start and end apart: 1, of which 1 were waited for; matrix products, arithmetic and copies ran while one was open for 0% of the time, Pallas kernels for 3%

profile of v1, /device:TPU:2, one launch (start us, length us, event | category | flops | bytes accessed | tf_op | source)
XLA Modules:
  0.0 73.0 jit_solution(1945253867591365778)
XLA Ops:
  0.0 0.0 copy-start.1
  0.0 2.9 %prepare_x.1 = (bf16[512,256]{1,0:T(8,128)(2,1)}, f32[48,4,128]{2,1,0:T(4,128)}) custom-call(f32[3,16,512]{2,1,0:T(8,128)} %bitcast.26, f32[16,2,512]{2,1,0:T(2,128)} %refs_1_.1, bf16[27,16,512]{2,1,0:T(8,128)(2,1)} %bitcast.14, s32[16,512]{1,0:T(8,128)} %refs_3_.1, bf16[4,4,512]{2,1,0:T(4,128)(2,1)} %refs_4_.1, s32[4,4]{1,0:T(4,128)} %refs_5_.1, ...), custom_call_target="tpu_custom_call" | custom-call | tf_op jit(solution)/shard_map/prepare_x/pallas_call | solution.py:438
  2.9 9.4 %all-to-all-start = ((bf16[32,16,256]{2,1,0:T(8,128)(2,1)}), bf16[32,16,256]{2,1,0:T(8,128)(2,1)S(1)}, u32[]{:S(2)}, u32[]{:S(2)}) async-start(bf16[32,16,256]{2,1,0:T(8,128)(2,1)} %bitcast.25), calls=%async_computation | async-start | bytes 524288 | tf_op jit(solution)/shard_map/all_to_all | solution.py:454
  12.3 0.0 copy-done.1
  12.4 2.1 %prepare_y.1 = (f32[216,8,128]{2,1,0:T(8,128)S(1)}, f32[216,128]{1,0:T(8,128)S(1)}, f32[56,128]{1,0:T(8,128)S(1)}, s32[8,128]{1,0:T(8,128)S(1)}) custom-call(s32[1]{0:T(128)} %bitcast.place, bf16[27,16,512]{2,1,0:T(8,128)(2,1)S(1)} %bitcast.23), custom_call_target="tpu_custom_call" | custom-call | tf_op jit(solution)/shard_map/prepare_y/pallas_call | solution.py:455
  14.5 0.0 copy-start
  14.5 5.7 %all-to-all-done = bf16[32,16,256]{2,1,0:T(8,128)(2,1)S(1)} async-done(((bf16[32,16,256]{2,1,0:T(8,128)(2,1)}), bf16[32,16,256]{2,1,0:T(8,128)(2,1)S(1)}, u32[]{:S(2)}, u32[]{:S(2)}) %all-to-all-start) | async-done | bytes 262176 | tf_op jit(solution)/shard_map/all_to_all | solution.py:454
  20.1 1.2 %solve_x.1 = bf16[512,128]{1,0:T(8,128)(2,1)S(1)} custom-call(bf16[512,256]{1,0:T(8,128)(2,1)S(1)} %bitcast.18), custom_call_target="tpu_custom_call" | custom-call | tf_op jit(solution)/shard_map/solve_x/pallas_call | solution.py:470
  21.3 0.0 copy-start.2
  21.3 11.5 %all_to_all.45 = bf16[32,16,128]{2,1,0:T(8,128)(2,1)S(1)} all-to-all(bf16[32,16,128]{2,1,0:T(8,128)(2,1)S(1)} %bitcast.22), channel_id=1, replica_groups=mesh['gx'=32,'gy'=16] {'gx'}, dimensions={0} | all-to-all | bytes 262144 | tf_op jit(solution)/shard_map/all_to_all | solution.py:485
  32.9 0.0 copy-done
  32.9 0.0 copy-done.2
  32.9 0.8 %finish_x.1 = (f32[288,128]{1,0:T(8,128)S(1)}, f32[24,8,128]{2,1,0:T(8,128)S(1)}, f32[48,128]{1,0:T(8,128)S(1)}) custom-call(bf16[512,128]{1,0:T(8,128)(2,1)S(1)} %bitcast.21, f32[48,4,128]{2,1,0:T(4,128)S(1)} %copy-done.2, bf16[27,16,512]{2,1,0:T(8,128)(2,1)S(1)} %bitcast.15, f32[216,8,128]{2,1,0:T(8,128)S(1)} %get-tuple-element.21.turned, ...), custom_call_target="tpu_custom_call" | custom-call | tf_op jit(solution)/shard_map/finish_x/pallas_call | solution.py:486
  33.7 10.6 %all_to_all.46 = f32[4,72,128]{2,1,0:T(8,128)S(1)} all-to-all(f32[4,72,128]{2,1,0:T(8,128)S(1)} %bitcast.24), channel_id=1, replica_groups={{0,1,2,3},{4,5,6,7},{8,9,10,11},{12,13,14,15},{16,17,18,19},{20,21,22,2..., dimensions={0} | all-to-all | bytes 294912 | tf_op jit(solution)/shard_map/all_to_all | solution.py:504
  44.2 0.1 join_y.1
  44.4 27.6 %all_to_all.47 = f32[4,72,128]{2,1,0:T(8,128)S(1)} all-to-all(f32[4,72,128]{2,1,0:T(8,128)S(1)} %bitcast.20), channel_id=1, replica_groups={{0,4,8,12},{1,5,9,13},{2,6,10,14},{3,7,11,15},{16,20,24,28},{17,21,25,2..., dimensions={0} | all-to-all | bytes 294912 | tf_op jit(solution)/shard_map/all_to_all | solution.py:513
  71.9 1.0 %finish_y.1 = f32[3,16,512]{2,1,0:T(8,128)} custom-call(s32[8,128]{1,0:T(8,128)S(1)} %get-tuple-element.16.spot, f32[288,128]{1,0:T(8,128)S(1)} %bitcast.17, f32[288,128]{1,0:T(8,128)S(1)} %bitcast.19, f32[24,8,128]{2,1,0:T(8,128)S(1)} %get-tuple-element.25.values, f32[48,128]{1,0:T(8,128)S(1)} %get-tuple-element.26.ends, ...), custom_call_target="tpu_custom_call" | custom-call | tf_op jit(solution)/shard_map/finish_y/pallas_call | solution.py:514
Async XLA Ops:
  0.0 12.4 %copy-start.1 = (bf16[16,27,512]{2,0,1:T(8,128)(2,1)S(1)}, bf16[16,27,512]{2,0,1:T(8,128)(2,1)}, u32[]{:S(2)}) copy-start(bf16[16,27,512]{2,0,1:T(8,128)(2,1)} %param.11) | copy-start | bytes 1327108
  2.9 17.2 %all-to-all-start = ((bf16[32,16,256]{2,1,0:T(8,128)(2,1)}), bf16[32,16,256]{2,1,0:T(8,128)(2,1)S(1)}, u32[]{:S(2)}, u32[]{:S(2)}) async-start(bf16[32,16,256]{2,1,0:T(8,128)(2,1)} %bitcast.25), calls=%async_computation | async-start | bytes 524288 | tf_op jit(solution)/shard_map/all_to_all | solution.py:454
  14.5 18.4 %copy-start = (bf16[16,27,512]{2,0,1:T(8,128)(2,1)S(1)}, bf16[16,27,512]{2,0,1:T(8,128)(2,1)}, u32[]{:S(2)}) copy-start(bf16[16,27,512]{2,0,1:T(8,128)(2,1)} %param.10) | copy-start | bytes 1327108
  21.3 11.5 %copy-start.2 = (f32[48,4,128]{2,1,0:T(4,128)S(1)}, f32[48,4,128]{2,1,0:T(4,128)}, u32[]{:S(2)}) copy-start(f32[48,4,128]{2,1,0:T(4,128)} %get-tuple-element.20.base) | copy-start | bytes 294916

commit v2 on v1

--- a/solution.py
+++ b/solution.py
@@ -9,8 +9,10 @@
 BF16 = jnp.bfloat16
 CX, CY, NZ = 16, 32, 16
 TX, TY = 32, 16
-NEAR = [[4 * q + k for k in range(4)] for q in range(4)]
-FAR = [[4 * q + k for q in range(4)] for k in range(4)]
+NEAR_ORDER, FAR_ORDER, TURN = (2, 3, 1, 0), (2, 3, 0, 1), 4
+NEAR = [[4 * q + k for k in NEAR_ORDER] for q in range(4)]
+FAR = [[4 * q + k for q in FAR_ORDER] for k in range(4)]
+LINE = [[(i - TURN) % TX for i in range(TX)]]
 ROWS = 72
 LANES = 128
 GROUPS = 4
@@ -52,6 +54,14 @@
                 fresh[i | bit] = jnp.where(low, pltpu.roll(first, LANES - bit * NZ, 1), second)
         parts = fresh
     return parts
+
+
+def halves(g):
+    return [((g * LANES + h * 64 + TURN * 16) % 512, slice(h * 64, h * 64 + 64)) for h in range(2)]
+
+
+def in_order(ref, g, first):
+    return jnp.concatenate([ref[at : at + 64, first : first + LANES].astype(F32) for at, _ in halves(g)], axis=0)
 
 
 def load_blocks(blocks, coef):
@@ -167,29 +177,30 @@
     routes = jnp.concatenate([routes] * 8, axis=0)
     lane = iota((LANES, LANES), 1)
     for g in range(GROUPS):
-        rows = slice(g * LANES, (g + 1) * LANES)
         slab = pan[:, g * LANES : (g + 1) * LANES]
         pieces = [pltpu.roll(slab, (112 - i * NZ) % LANES, 1) if i < 7 else slab for i in range(8)]
         first = feats[pl.ds(g * 256, LANES), :].T
         first = jnp.where(lane >= 112, jnp.concatenate(pieces, axis=0), first)
-        packed[rows, 0:LANES] = first.astype(BF16)
+        for at, part in halves(g):
+            packed[at : at + 64, 0:LANES] = first[part, :].astype(BF16)
         second = feats[pl.ds(g * 256 + LANES, LANES), :].T
         second = jnp.where(lane == 72, routes, second)
-        packed[rows, LANES : 2 * LANES] = second.astype(BF16)
+        for at, part in halves(g):
+            packed[at : at + 64, LANES : 2 * LANES] = second[part, :].astype(BF16)
 
 
 def solve_x(received, answer, low, high, spread, target, out):
     for g in range(GROUPS):
         rows = slice(g * LANES, (g + 1) * LANES)
-        low[rows, :] = received[rows, 0:LANES].astype(F32).T
-        high[rows, :] = received[rows, LANES : 2 * LANES].astype(F32).T
+        low[rows, :] = in_order(received, g, 0).T
+        high[rows, :] = in_order(received, g, LANES).T
     r_id, c_id = iota((LANES, LANES), 0), iota((LANES, LANES), 1)
     lane = iota((512, LANES), 1)
     copy_panel = ((r_id >= 112) & ((r_id - 112) == (c_id & (NZ - 1)))).astype(F32).astype(BF16)
     copy_route = (r_id == 72).astype(F32).astype(BF16)
-    panel_part = received[:, 0:LANES].astype(F32)
+    panel_part = jnp.concatenate([in_order(received, g, 0) for g in range(GROUPS)], axis=0)
     panel_part = jnp.where(lane >= 112, panel_part, 0.0).astype(BF16)
-    route_part = received[:, LANES : 2 * LANES].astype(F32)
+    route_part = jnp.concatenate([in_order(received, g, LANES) for g in range(GROUPS)], axis=0)
     route_part = jnp.where(lane == 72, route_part, 0.0).astype(BF16)
     spread[...] = jnp.dot(panel_part, copy_panel, preferred_element_type=F32)
     target[...] = jnp.dot(route_part, copy_route, preferred_element_type=F32)
@@ -258,7 +269,9 @@
             v = v - part
     for g in range(GROUPS):
         rows = slice(g * LANES, (g + 1) * LANES)
-        answer[rows, :] = out[rows, :].T.astype(BF16)
+        turned_out = out[rows, :].T.astype(BF16)
+        for at, part in halves(g):
+            answer[at : at + 64, :] = turned_out[part, :]
 
 
 def prepare_y(place, blocks, turned, parts, whole, spot, plain, coef):
@@ -298,7 +311,7 @@
     load_blocks(blocks, coef)
     for g in range(GROUPS):
         rows = slice(g * LANES, (g + 1) * LANES)
-        low[rows, :] = received[rows, :].astype(F32).T
+        low[rows, :] = in_order(received, g, 0).T
 
     def entry(k):
         rows = [low[pl.ds(piece * 6 + k, GROUPS, stride=LANES), :] for piece in range(3)]
@@ -356,15 +369,16 @@
         sent[pl.ds(i * ROWS, ROWS), :] = sent[pl.ds(0, ROWS), :]
 
 
-def get_map(ref, i):
+def get_map(ref, order, i):
+    i = order.index(i)
     v = [ref[pl.ds(i * ROWS + k * 2, 2), :] for k in range(MAP)]
     return v[0:9], v[9:18], v[18:27], v[27:30], v[30:33]
 
 
 def join_y(received, sent):
-    a, c, d, b, e = get_map(received, 0)
+    a, c, d, b, e = get_map(received, NEAR_ORDER, 0)
     for i in range(1, 4):
-        a1, c1, d1, b1, e1 = get_map(received, i)
+        a1, c1, d1, b1, e1 = get_map(received, NEAR_ORDER, i)
         e = add(mv(c, add(mv(d1, b), e1)), e)
         d = add(mm(c, mm(d1, a)), d)
         b = add(mv(a1, b), b1)
@@ -373,8 +387,8 @@
     put_map(sent, a + c + d + b + e)
 
 
-def narrow(received, mine, enter, finish):
-    maps = [get_map(received, i) for i in range(4)]
+def narrow(received, order, mine, enter, finish):
+    maps = [get_map(received, order, i) for i in range(4)]
     fs = [enter]
     for i in range(3):
         fs.append(add(mv(maps[i][0], fs[i]), maps[i][3]))
@@ -392,8 +406,8 @@
 def finish_y(spot, near, far, values, ends, turned, parts, result, edge):
     me = spot[0:2, :]
     zero = [jnp.zeros((2, LANES), F32) for _ in range(3)]
-    enter, finish = narrow(far, me // 4, zero, zero)
-    enter, finish = narrow(near, me % 4, enter, finish)
+    enter, finish = narrow(far, FAR_ORDER, me // 4, zero, zero)
+    enter, finish = narrow(near, NEAR_ORDER, me % 4, enter, finish)
     f = enter
     inside = []
     for l in range(GROUPS):
@@ -451,7 +465,7 @@
         ],
         name="prepare_x",
     )(*inputs)
-    received = lax.all_to_all(packed, "gx", split_axis=0, concat_axis=0, tiled=True)
+    received = lax.all_to_all(packed, "gx", split_axis=0, concat_axis=0, tiled=True, axis_index_groups=LINE)
     turned, parts, whole, spot = pl.pallas_call(
         prepare_y,
         out_shape=(
@@ -482,7 +496,7 @@
         compiler_params=PARAMS,
         name="solve_x",
     )(received)
-    entries = lax.all_to_all(answer, "gx", split_axis=0, concat_axis=0, tiled=True)
+    entries = lax.all_to_all(answer, "gx", split_axis=0, concat_axis=0, tiled=True, axis_index_groups=LINE)
     sent, values, ends = pl.pallas_call(
         finish_x,
         out_shape=(

time: 73.3 us -> 62.7 us (0.86)
  the two profiles are of different devices: /device:TPU:2 before, /device:TPU:4 now
where the time goes in v2:
time: 62.7 us; the launch traced here: 62.4 us
  blocking collectives  39.6 us (63%)
  starting transfers between devices  10 us (16%)
  Pallas kernels  8.1 us (13%)
  waiting for transfers between devices  4.59 us (7%)
    all_to_all x1, blocking collectives, body(): lax.all_to_all(joined, 'gy', split_axis=0, concat_axis=0, tiled=True, axi...  19.7 us
    all_to_all x1, blocking collectives, body(): lax.all_to_all(answer, 'gx', split_axis=0, concat_axis=0, tiled=True, axi...  11.4 us
    all_to_all x1, starting transfers between devices, body(): lax.all_to_all(packed, 'gx', split_axis=0, concat_axis=0, tiled=True, axi...  10 us
    all_to_all x1, blocking collectives, body(): lax.all_to_all(sent, 'gy', split_axis=0, concat_axis=0, tiled=True, axis_...  8.49 us
    all_to_all x1, waiting for transfers between devices, body(): lax.all_to_all(packed, 'gx', split_axis=0, concat_axis=0, tiled=True, axi...  4.59 us
    pallas_call x1, Pallas kernels, body(): pl.pallas_call(prepare_x, out_shape=(shape((512, 256), BF16), shape((CX *...  2.88 us
    pallas_call x1, Pallas kernels, body(): pl.pallas_call(prepare_y, out_shape=(shape((8 * 27, 8, LANES), F32), shap...  2.09 us
  transfers between devices with their start and end apart: 1, of which 1 were waited for; matrix products, arithmetic and copies ran while one was open for 0% of the time, Pallas kernels for 3%

profile of v2, /device:TPU:4, one launch (start us, length us, event | category | flops | bytes accessed | tf_op | source)
XLA Modules:
  0.0 62.4 jit_solution(1993796993473642406)
XLA Ops:
  0.0 0.0 copy-start.1
  0.0 2.9 %prepare_x.1 = (bf16[512,256]{1,0:T(8,128)(2,1)}, f32[48,4,128]{2,1,0:T(4,128)}) custom-call(f32[3,16,512]{2,1,0:T(8,128)} %bitcast.26, f32[16,2,512]{2,1,0:T(2,128)} %refs_1_.1, bf16[27,16,512]{2,1,0:T(8,128)(2,1)} %bitcast.14, s32[16,512]{1,0:T(8,128)} %refs_3_.1, bf16[4,4,512]{2,1,0:T(4,128)(2,1)} %refs_4_.1, s32[4,4]{1,0:T(4,128)} %refs_5_.1, ...), custom_call_target="tpu_custom_call" | custom-call | tf_op jit(solution)/shard_map/prepare_x/pallas_call | solution.py:452
  2.9 10.0 %all-to-all-start = ((bf16[32,16,256]{2,1,0:T(8,128)(2,1)}), bf16[32,16,256]{2,1,0:T(8,128)(2,1)S(1)}, u32[]{:S(2)}, u32[]{:S(2)}) async-start(bf16[32,16,256]{2,1,0:T(8,128)(2,1)} %bitcast.25), calls=%async_computation | async-start | bytes 524288 | tf_op jit(solution)/shard_map/all_to_all | solution.py:468
  12.9 0.0 copy-done.1
  12.9 2.1 %prepare_y.1 = (f32[216,8,128]{2,1,0:T(8,128)S(1)}, f32[216,128]{1,0:T(8,128)S(1)}, f32[56,128]{1,0:T(8,128)S(1)}, s32[8,128]{1,0:T(8,128)S(1)}) custom-call(s32[1]{0:T(128)} %bitcast.place, bf16[27,16,512]{2,1,0:T(8,128)(2,1)S(1)} %bitcast.23), custom_call_target="tpu_custom_call" | custom-call | tf_op jit(solution)/shard_map/prepare_y/pallas_call | solution.py:469
  15.0 0.0 copy-start
  15.0 4.6 %all-to-all-done = bf16[32,16,256]{2,1,0:T(8,128)(2,1)S(1)} async-done(((bf16[32,16,256]{2,1,0:T(8,128)(2,1)}), bf16[32,16,256]{2,1,0:T(8,128)(2,1)S(1)}, u32[]{:S(2)}, u32[]{:S(2)}) %all-to-all-start) | async-done | bytes 262176 | tf_op jit(solution)/shard_map/all_to_all | solution.py:468
  19.6 1.2 %solve_x.1 = bf16[512,128]{1,0:T(8,128)(2,1)S(1)} custom-call(bf16[512,256]{1,0:T(8,128)(2,1)S(1)} %bitcast.18), custom_call_target="tpu_custom_call" | custom-call | tf_op jit(solution)/shard_map/solve_x/pallas_call | solution.py:484
  20.8 0.0 copy-start.2
  20.8 11.4 %all_to_all.45 = bf16[32,16,128]{2,1,0:T(8,128)(2,1)S(1)} all-to-all(bf16[32,16,128]{2,1,0:T(8,128)(2,1)S(1)} %bitcast.22), channel_id=1, replica_groups={{448,464,480,496,0,16,32,48,64,80,96,112,128,144,160,176,192,208,224,24..., dimensions={0} | all-to-all | bytes 262144 | tf_op jit(solution)/shard_map/all_to_all | solution.py:499
  32.3 0.0 copy-done
  32.3 0.0 copy-done.2
  32.3 0.8 %finish_x.1 = (f32[288,128]{1,0:T(8,128)S(1)}, f32[24,8,128]{2,1,0:T(8,128)S(1)}, f32[48,128]{1,0:T(8,128)S(1)}) custom-call(bf16[512,128]{1,0:T(8,128)(2,1)S(1)} %bitcast.21, f32[48,4,128]{2,1,0:T(4,128)S(1)} %copy-done.2, bf16[27,16,512]{2,1,0:T(8,128)(2,1)S(1)} %bitcast.15, f32[216,8,128]{2,1,0:T(8,128)S(1)} %get-tuple-element.21.turned, ...), custom_call_target="tpu_custom_call" | custom-call | tf_op jit(solution)/shard_map/finish_x/pallas_call | solution.py:500
  33.0 8.5 %all_to_all.46 = f32[4,72,128]{2,1,0:T(8,128)S(1)} all-to-all(f32[4,72,128]{2,1,0:T(8,128)S(1)} %bitcast.24), channel_id=1, replica_groups={{2,3,1,0},{6,7,5,4},{10,11,9,8},{14,15,13,12},{18,19,17,16},{22,23,21,2..., dimensions={0} | all-to-all | bytes 294912 | tf_op jit(solution)/shard_map/all_to_all | solution.py:518
  41.5 0.1 join_y.1
  41.7 19.7 %all_to_all.47 = f32[4,72,128]{2,1,0:T(8,128)S(1)} all-to-all(f32[4,72,128]{2,1,0:T(8,128)S(1)} %bitcast.20), channel_id=1, replica_groups={{8,12,0,4},{9,13,1,5},{10,14,2,6},{11,15,3,7},{24,28,16,20},{25,29,17,2..., dimensions={0} | all-to-all | bytes 294912 | tf_op jit(solution)/shard_map/all_to_all | solution.py:527
  61.3 1.0 %finish_y.1 = f32[3,16,512]{2,1,0:T(8,128)} custom-call(s32[8,128]{1,0:T(8,128)S(1)} %get-tuple-element.16.spot, f32[288,128]{1,0:T(8,128)S(1)} %bitcast.17, f32[288,128]{1,0:T(8,128)S(1)} %bitcast.19, f32[24,8,128]{2,1,0:T(8,128)S(1)} %get-tuple-element.25.values, f32[48,128]{1,0:T(8,128)S(1)} %get-tuple-element.26.ends, ...), custom_call_target="tpu_custom_call" | custom-call | tf_op jit(solution)/shard_map/finish_y/pallas_call | solution.py:528
Async XLA Ops:
  0.0 12.9 %copy-start.1 = (bf16[16,27,512]{2,0,1:T(8,128)(2,1)S(1)}, bf16[16,27,512]{2,0,1:T(8,128)(2,1)}, u32[]{:S(2)}) copy-start(bf16[16,27,512]{2,0,1:T(8,128)(2,1)} %param.11) | copy-start | bytes 1327108
  2.9 16.7 %all-to-all-start = ((bf16[32,16,256]{2,1,0:T(8,128)(2,1)}), bf16[32,16,256]{2,1,0:T(8,128)(2,1)S(1)}, u32[]{:S(2)}, u32[]{:S(2)}) async-start(bf16[32,16,256]{2,1,0:T(8,128)(2,1)} %bitcast.25), calls=%async_computation | async-start | bytes 524288 | tf_op jit(solution)/shard_map/all_to_all | solution.py:468
  15.0 17.2 %copy-start = (bf16[16,27,512]{2,0,1:T(8,128)(2,1)S(1)}, bf16[16,27,512]{2,0,1:T(8,128)(2,1)}, u32[]{:S(2)}) copy-start(bf16[16,27,512]{2,0,1:T(8,128)(2,1)} %param.10) | copy-start | bytes 1327108
  20.8 11.5 %copy-start.2 = (f32[48,4,128]{2,1,0:T(4,128)S(1)}, f32[48,4,128]{2,1,0:T(4,128)}, u32[]{:S(2)}) copy-start(f32[48,4,128]{2,1,0:T(4,128)} %get-tuple-element.20.base) | copy-start | bytes 294916

commit v3 on v2

--- a/solution.py
+++ b/solution.py
@@ -9,7 +9,7 @@
 BF16 = jnp.bfloat16
 CX, CY, NZ = 16, 32, 16
 TX, TY = 32, 16
-NEAR_ORDER, FAR_ORDER, TURN = (2, 3, 1, 0), (2, 3, 0, 1), 4
+NEAR_ORDER, FAR_ORDER, TURN = (1, 2, 3, 0), (2, 3, 0, 1), 4
 NEAR = [[4 * q + k for k in NEAR_ORDER] for q in range(4)]
 FAR = [[4 * q + k for q in FAR_ORDER] for k in range(4)]
 LINE = [[(i - TURN) % TX for i in range(TX)]]
@@ -107,7 +107,7 @@
         base[x * 3 + 1] = field[1] + inflow - outflow + 0.2 * depth(field[1], z)
         base[x * 3 + 2] = field[2] + outflow + 0.2 * depth(field[2], z)
     for g in range(GROUPS):
-        feats[pl.ds(g * 256 + 96, 160), :] = jnp.zeros((160, LANES), F32)
+        feats[pl.ds(g * 256 + 192, 64), :] = jnp.zeros((64, LANES), F32)
     copies[2].wait()
     load_blocks(blocks, coef)
     copies[3].wait()

time: 62.7 us -> 62.3 us (level)
  the two profiles are of different devices: /device:TPU:4 before, /device:TPU:1 now
where the time goes in v3:
time: 62.3 us; the launch traced here: 61.2 us
  blocking collectives  36.7 us (59%)
  starting transfers between devices  13.6 us (22%)
  Pallas kernels  8.08 us (13%)
  waiting for transfers between devices  2.7 us (4%)
    all_to_all x1, blocking collectives, body(): lax.all_to_all(joined, 'gy', split_axis=0, concat_axis=0, tiled=True, axi...  18.9 us
    all_to_all x1, starting transfers between devices, body(): lax.all_to_all(packed, 'gx', split_axis=0, concat_axis=0, tiled=True, axi...  13.6 us
    all_to_all x1, blocking collectives, body(): lax.all_to_all(answer, 'gx', split_axis=0, concat_axis=0, tiled=True, axi...  10.9 us
    all_to_all x1, blocking collectives, body(): lax.all_to_all(sent, 'gy', split_axis=0, concat_axis=0, tiled=True, axis_...  6.97 us
    pallas_call x1, Pallas kernels, body(): pl.pallas_call(prepare_x, out_shape=(shape((512, 256), BF16), shape((CX *...  2.87 us
    all_to_all x1, waiting for transfers between devices, body(): lax.all_to_all(packed, 'gx', split_axis=0, concat_axis=0, tiled=True, axi...  2.7 us
    pallas_call x1, Pallas kernels, body(): pl.pallas_call(prepare_y, out_shape=(shape((8 * 27, 8, LANES), F32), shap...  2.09 us
  transfers between devices with their start and end apart: 1, of which 1 were waited for; matrix products, arithmetic and copies ran while one was open for 0% of the time, Pallas kernels for 3%

profile of v3, /device:TPU:1, one launch (start us, length us, event | category | flops | bytes accessed | tf_op | source)
XLA Modules:
  0.0 61.2 jit_solution(12802474018420911412)
XLA Ops:
  0.0 0.0 copy-start.1
  0.0 2.9 %prepare_x.1 = (bf16[512,256]{1,0:T(8,128)(2,1)}, f32[48,4,128]{2,1,0:T(4,128)}) custom-call(f32[3,16,512]{2,1,0:T(8,128)} %bitcast.26, f32[16,2,512]{2,1,0:T(2,128)} %refs_1_.1, bf16[27,16,512]{2,1,0:T(8,128)(2,1)} %bitcast.14, s32[16,512]{1,0:T(8,128)} %refs_3_.1, bf16[4,4,512]{2,1,0:T(4,128)(2,1)} %refs_4_.1, s32[4,4]{1,0:T(4,128)} %refs_5_.1, ...), custom_call_target="tpu_custom_call" | custom-call | tf_op jit(solution)/shard_map/prepare_x/pallas_call | solution.py:452
  2.9 13.6 %all-to-all-start = ((bf16[32,16,256]{2,1,0:T(8,128)(2,1)}), bf16[32,16,256]{2,1,0:T(8,128)(2,1)S(1)}, u32[]{:S(2)}, u32[]{:S(2)}) async-start(bf16[32,16,256]{2,1,0:T(8,128)(2,1)} %bitcast.25), calls=%async_computation | async-start | bytes 524288 | tf_op jit(solution)/shard_map/all_to_all | solution.py:468
  16.5 0.0 copy-done.1
  16.5 2.1 %prepare_y.1 = (f32[216,8,128]{2,1,0:T(8,128)S(1)}, f32[216,128]{1,0:T(8,128)S(1)}, f32[56,128]{1,0:T(8,128)S(1)}, s32[8,128]{1,0:T(8,128)S(1)}) custom-call(s32[1]{0:T(128)} %bitcast.place, bf16[27,16,512]{2,1,0:T(8,128)(2,1)S(1)} %bitcast.23), custom_call_target="tpu_custom_call" | custom-call | tf_op jit(solution)/shard_map/prepare_y/pallas_call | solution.py:469
  18.6 0.0 copy-start
  18.6 2.7 %all-to-all-done = bf16[32,16,256]{2,1,0:T(8,128)(2,1)S(1)} async-done(((bf16[32,16,256]{2,1,0:T(8,128)(2,1)}), bf16[32,16,256]{2,1,0:T(8,128)(2,1)S(1)}, u32[]{:S(2)}, u32[]{:S(2)}) %all-to-all-start) | async-done | bytes 262176 | tf_op jit(solution)/shard_map/all_to_all | solution.py:468
  21.3 1.2 %solve_x.1 = bf16[512,128]{1,0:T(8,128)(2,1)S(1)} custom-call(bf16[512,256]{1,0:T(8,128)(2,1)S(1)} %bitcast.18), custom_call_target="tpu_custom_call" | custom-call | tf_op jit(solution)/shard_map/solve_x/pallas_call | solution.py:484
  22.5 0.0 copy-start.2
  22.5 10.9 %all_to_all.45 = bf16[32,16,128]{2,1,0:T(8,128)(2,1)S(1)} all-to-all(bf16[32,16,128]{2,1,0:T(8,128)(2,1)S(1)} %bitcast.22), channel_id=1, replica_groups={{448,464,480,496,0,16,32,48,64,80,96,112,128,144,160,176,192,208,224,24..., dimensions={0} | all-to-all | bytes 262144 | tf_op jit(solution)/shard_map/all_to_all | solution.py:499
  33.4 0.0 copy-done
  33.4 0.0 copy-done.2
  33.4 0.8 %finish_x.1 = (f32[288,128]{1,0:T(8,128)S(1)}, f32[24,8,128]{2,1,0:T(8,128)S(1)}, f32[48,128]{1,0:T(8,128)S(1)}) custom-call(bf16[512,128]{1,0:T(8,128)(2,1)S(1)} %bitcast.21, f32[48,4,128]{2,1,0:T(4,128)S(1)} %copy-done.2, bf16[27,16,512]{2,1,0:T(8,128)(2,1)S(1)} %bitcast.15, f32[216,8,128]{2,1,0:T(8,128)S(1)} %get-tuple-element.21.turned, ...), custom_call_target="tpu_custom_call" | custom-call | tf_op jit(solution)/shard_map/finish_x/pallas_call | solution.py:500
  34.2 7.0 %all_to_all.46 = f32[4,72,128]{2,1,0:T(8,128)S(1)} all-to-all(f32[4,72,128]{2,1,0:T(8,128)S(1)} %bitcast.24), channel_id=1, replica_groups={{1,2,3,0},{5,6,7,4},{9,10,11,8},{13,14,15,12},{17,18,19,16},{21,22,23,2..., dimensions={0} | all-to-all | bytes 294912 | tf_op jit(solution)/shard_map/all_to_all | solution.py:518
  41.2 0.1 join_y.1
  41.3 18.9 %all_to_all.47 = f32[4,72,128]{2,1,0:T(8,128)S(1)} all-to-all(f32[4,72,128]{2,1,0:T(8,128)S(1)} %bitcast.20), channel_id=1, replica_groups={{8,12,0,4},{9,13,1,5},{10,14,2,6},{11,15,3,7},{24,28,16,20},{25,29,17,2..., dimensions={0} | all-to-all | bytes 294912 | tf_op jit(solution)/shard_map/all_to_all | solution.py:527
  60.2 1.0 %finish_y.1 = f32[3,16,512]{2,1,0:T(8,128)} custom-call(s32[8,128]{1,0:T(8,128)S(1)} %get-tuple-element.16.spot, f32[288,128]{1,0:T(8,128)S(1)} %bitcast.17, f32[288,128]{1,0:T(8,128)S(1)} %bitcast.19, f32[24,8,128]{2,1,0:T(8,128)S(1)} %get-tuple-element.25.values, f32[48,128]{1,0:T(8,128)S(1)} %get-tuple-element.26.ends, ...), custom_call_target="tpu_custom_call" | custom-call | tf_op jit(solution)/shard_map/finish_y/pallas_call | solution.py:528
Async XLA Ops:
  0.0 16.5 %copy-start.1 = (bf16[16,27,512]{2,0,1:T(8,128)(2,1)S(1)}, bf16[16,27,512]{2,0,1:T(8,128)(2,1)}, u32[]{:S(2)}) copy-start(bf16[16,27,512]{2,0,1:T(8,128)(2,1)} %param.11) | copy-start | bytes 1327108
  2.9 18.4 %all-to-all-start = ((bf16[32,16,256]{2,1,0:T(8,128)(2,1)}), bf16[32,16,256]{2,1,0:T(8,128)(2,1)S(1)}, u32[]{:S(2)}, u32[]{:S(2)}) async-start(bf16[32,16,256]{2,1,0:T(8,128)(2,1)} %bitcast.25), calls=%async_computation | async-start | bytes 524288 | tf_op jit(solution)/shard_map/all_to_all | solution.py:468
  18.6 14.8 %copy-start = (bf16[16,27,512]{2,0,1:T(8,128)(2,1)S(1)}, bf16[16,27,512]{2,0,1:T(8,128)(2,1)}, u32[]{:S(2)}) copy-start(bf16[16,27,512]{2,0,1:T(8,128)(2,1)} %param.10) | copy-start | bytes 1327108
  22.5 10.9 %copy-start.2 = (f32[48,4,128]{2,1,0:T(4,128)S(1)}, f32[48,4,128]{2,1,0:T(4,128)}, u32[]{:S(2)}) copy-start(f32[48,4,128]{2,1,0:T(4,128)} %get-tuple-element.20.base) | copy-start | bytes 294916

commit v4 on v3

--- a/solution.py
+++ b/solution.py
@@ -9,7 +9,7 @@
 BF16 = jnp.bfloat16
 CX, CY, NZ = 16, 32, 16
 TX, TY = 32, 16
-NEAR_ORDER, FAR_ORDER, TURN = (1, 2, 3, 0), (2, 3, 0, 1), 4
+NEAR_ORDER, FAR_ORDER, TURN = (1, 2, 3, 0), (2, 1, 0, 3), 12
 NEAR = [[4 * q + k for k in NEAR_ORDER] for q in range(4)]
 FAR = [[4 * q + k for q in FAR_ORDER] for k in range(4)]
 LINE = [[(i - TURN) % TX for i in range(TX)]]

time: 62.3 us -> 61.8 us (level); the launches traced: 61.2 us -> 61.5 us
  blocking collectives: 36.7 us -> 37.4 us
  waiting for transfers between devices: 2.7 us -> 2.01 us
    all_to_all x1, blocking collectives: 18.9 us -> 19.7 us  [body(): lax.all_to_all(joined, 'gy', split_axis=0, concat_axis=0, tiled=True, axi...]
    all_to_all x1, waiting for transfers between devices: 2.7 us -> 2.01 us  [body(): lax.all_to_all(packed, 'gx', split_axis=0, concat_axis=0, tiled=True, axi...]
where the time goes in v4:
time: 61.8 us; the launch traced here: 61.5 us
  blocking collectives  37.4 us (61%)
  starting transfers between devices  13.9 us (22%)
  Pallas kernels  8.08 us (13%)
  waiting for transfers between devices  2.01 us (3%)
    all_to_all x1, blocking collectives, body(): lax.all_to_all(joined, 'gy', split_axis=0, concat_axis=0, tiled=True, axi...  19.7 us
    all_to_all x1, starting transfers between devices, body(): lax.all_to_all(packed, 'gx', split_axis=0, concat_axis=0, tiled=True, axi...  13.9 us
    all_to_all x1, blocking collectives, body(): lax.all_to_all(answer, 'gx', split_axis=0, concat_axis=0, tiled=True, axi...  10.8 us
    all_to_all x1, blocking collectives, body(): lax.all_to_all(sent, 'gy', split_axis=0, concat_axis=0, tiled=True, axis_...  6.97 us
    pallas_call x1, Pallas kernels, body(): pl.pallas_call(prepare_x, out_shape=(shape((512, 256), BF16), shape((CX *...  2.87 us
    pallas_call x1, Pallas kernels, body(): pl.pallas_call(prepare_y, out_shape=(shape((8 * 27, 8, LANES), F32), shap...  2.09 us
    all_to_all x1, waiting for transfers between devices, body(): lax.all_to_all(packed, 'gx', split_axis=0, concat_axis=0, tiled=True, axi...  2.01 us
  transfers between devices with their start and end apart: 1, of which 1 were waited for; matrix products, arithmetic and copies ran while one was open for 0% of the time, Pallas kernels for 3%

profile of v4, /device:TPU:1, one launch (start us, length us, event | category | flops | bytes accessed | tf_op | source)
XLA Modules:
  0.0 61.5 jit_solution(18118588094560115787)
XLA Ops:
  0.0 0.0 copy-start.1
  0.0 2.9 %prepare_x.1 = (bf16[512,256]{1,0:T(8,128)(2,1)}, f32[48,4,128]{2,1,0:T(4,128)}) custom-call(f32[3,16,512]{2,1,0:T(8,128)} %bitcast.26, f32[16,2,512]{2,1,0:T(2,128)} %refs_1_.1, bf16[27,16,512]{2,1,0:T(8,128)(2,1)} %bitcast.14, s32[16,512]{1,0:T(8,128)} %refs_3_.1, bf16[4,4,512]{2,1,0:T(4,128)(2,1)} %refs_4_.1, s32[4,4]{1,0:T(4,128)} %refs_5_.1, ...), custom_call_target="tpu_custom_call" | custom-call | tf_op jit(solution)/shard_map/prepare_x/pallas_call | solution.py:452
  2.9 13.9 %all-to-all-start = ((bf16[32,16,256]{2,1,0:T(8,128)(2,1)}), bf16[32,16,256]{2,1,0:T(8,128)(2,1)S(1)}, u32[]{:S(2)}, u32[]{:S(2)}) async-start(bf16[32,16,256]{2,1,0:T(8,128)(2,1)} %bitcast.25), calls=%async_computation | async-start | bytes 524288 | tf_op jit(solution)/shard_map/all_to_all | solution.py:468
  16.8 0.0 copy-done.1
  16.8 2.1 %prepare_y.1 = (f32[216,8,128]{2,1,0:T(8,128)S(1)}, f32[216,128]{1,0:T(8,128)S(1)}, f32[56,128]{1,0:T(8,128)S(1)}, s32[8,128]{1,0:T(8,128)S(1)}) custom-call(s32[1]{0:T(128)} %bitcast.place, bf16[27,16,512]{2,1,0:T(8,128)(2,1)S(1)} %bitcast.23), custom_call_target="tpu_custom_call" | custom-call | tf_op jit(solution)/shard_map/prepare_y/pallas_call | solution.py:469
  18.9 0.0 copy-start
  18.9 2.0 %all-to-all-done = bf16[32,16,256]{2,1,0:T(8,128)(2,1)S(1)} async-done(((bf16[32,16,256]{2,1,0:T(8,128)(2,1)}), bf16[32,16,256]{2,1,0:T(8,128)(2,1)S(1)}, u32[]{:S(2)}, u32[]{:S(2)}) %all-to-all-start) | async-done | bytes 262176 | tf_op jit(solution)/shard_map/all_to_all | solution.py:468
  20.9 1.2 %solve_x.1 = bf16[512,128]{1,0:T(8,128)(2,1)S(1)} custom-call(bf16[512,256]{1,0:T(8,128)(2,1)S(1)} %bitcast.18), custom_call_target="tpu_custom_call" | custom-call | tf_op jit(solution)/shard_map/solve_x/pallas_call | solution.py:484
  22.1 0.0 copy-start.2
  22.1 10.8 %all_to_all.45 = bf16[32,16,128]{2,1,0:T(8,128)(2,1)S(1)} all-to-all(bf16[32,16,128]{2,1,0:T(8,128)(2,1)S(1)} %bitcast.22), channel_id=1, replica_groups={{320,336,352,368,384,400,416,432,448,464,480,496,0,16,32,48,64,80,96,11..., dimensions={0} | all-to-all | bytes 262144 | tf_op jit(solution)/shard_map/all_to_all | solution.py:499
  32.9 0.0 copy-done
  32.9 0.0 copy-done.2
  32.9 0.8 %finish_x.1 = (f32[288,128]{1,0:T(8,128)S(1)}, f32[24,8,128]{2,1,0:T(8,128)S(1)}, f32[48,128]{1,0:T(8,128)S(1)}) custom-call(bf16[512,128]{1,0:T(8,128)(2,1)S(1)} %bitcast.21, f32[48,4,128]{2,1,0:T(4,128)S(1)} %copy-done.2, bf16[27,16,512]{2,1,0:T(8,128)(2,1)S(1)} %bitcast.15, f32[216,8,128]{2,1,0:T(8,128)S(1)} %get-tuple-element.21.turned, ...), custom_call_target="tpu_custom_call" | custom-call | tf_op jit(solution)/shard_map/finish_x/pallas_call | solution.py:500
  33.7 7.0 %all_to_all.46 = f32[4,72,128]{2,1,0:T(8,128)S(1)} all-to-all(f32[4,72,128]{2,1,0:T(8,128)S(1)} %bitcast.24), channel_id=1, replica_groups={{1,2,3,0},{5,6,7,4},{9,10,11,8},{13,14,15,12},{17,18,19,16},{21,22,23,2..., dimensions={0} | all-to-all | bytes 294912 | tf_op jit(solution)/shard_map/all_to_all | solution.py:518
  40.7 0.1 join_y.1
  40.8 19.7 %all_to_all.47 = f32[4,72,128]{2,1,0:T(8,128)S(1)} all-to-all(f32[4,72,128]{2,1,0:T(8,128)S(1)} %bitcast.20), channel_id=1, replica_groups={{8,4,0,12},{9,5,1,13},{10,6,2,14},{11,7,3,15},{24,20,16,28},{25,21,17,2..., dimensions={0} | all-to-all | bytes 294912 | tf_op jit(solution)/shard_map/all_to_all | solution.py:527
  60.5 1.0 %finish_y.1 = f32[3,16,512]{2,1,0:T(8,128)} custom-call(s32[8,128]{1,0:T(8,128)S(1)} %get-tuple-element.16.spot, f32[288,128]{1,0:T(8,128)S(1)} %bitcast.17, f32[288,128]{1,0:T(8,128)S(1)} %bitcast.19, f32[24,8,128]{2,1,0:T(8,128)S(1)} %get-tuple-element.25.values, f32[48,128]{1,0:T(8,128)S(1)} %get-tuple-element.26.ends, ...), custom_call_target="tpu_custom_call" | custom-call | tf_op jit(solution)/shard_map/finish_y/pallas_call | solution.py:528
Async XLA Ops:
  0.0 16.8 %copy-start.1 = (bf16[16,27,512]{2,0,1:T(8,128)(2,1)S(1)}, bf16[16,27,512]{2,0,1:T(8,128)(2,1)}, u32[]{:S(2)}) copy-start(bf16[16,27,512]{2,0,1:T(8,128)(2,1)} %param.11) | copy-start | bytes 1327108
  2.9 18.0 %all-to-all-start = ((bf16[32,16,256]{2,1,0:T(8,128)(2,1)}), bf16[32,16,256]{2,1,0:T(8,128)(2,1)S(1)}, u32[]{:S(2)}, u32[]{:S(2)}) async-start(bf16[32,16,256]{2,1,0:T(8,128)(2,1)} %bitcast.25), calls=%async_computation | async-start | bytes 524288 | tf_op jit(solution)/shard_map/all_to_all | solution.py:468
  18.9 14.0 %copy-start = (bf16[16,27,512]{2,0,1:T(8,128)(2,1)S(1)}, bf16[16,27,512]{2,0,1:T(8,128)(2,1)}, u32[]{:S(2)}) copy-start(bf16[16,27,512]{2,0,1:T(8,128)(2,1)} %param.10) | copy-start | bytes 1327108
  22.1 10.8 %copy-start.2 = (f32[48,4,128]{2,1,0:T(4,128)S(1)}, f32[48,4,128]{2,1,0:T(4,128)}, u32[]{:S(2)}) copy-start(f32[48,4,128]{2,1,0:T(4,128)} %get-tuple-element.20.base) | copy-start | bytes 294916

commit v5 on v4

--- a/solution.py
+++ b/solution.py
@@ -190,17 +190,19 @@
 
 
 def solve_x(received, answer, low, high, spread, target, out):
+    firsts = [in_order(received, g, 0) for g in range(GROUPS)]
+    seconds = [in_order(received, g, LANES) for g in range(GROUPS)]
     for g in range(GROUPS):
         rows = slice(g * LANES, (g + 1) * LANES)
-        low[rows, :] = in_order(received, g, 0).T
-        high[rows, :] = in_order(received, g, LANES).T
+        low[rows, :] = firsts[g].T
+        high[rows, :] = seconds[g].T
     r_id, c_id = iota((LANES, LANES), 0), iota((LANES, LANES), 1)
     lane = iota((512, LANES), 1)
     copy_panel = ((r_id >= 112) & ((r_id - 112) == (c_id & (NZ - 1)))).astype(F32).astype(BF16)
     copy_route = (r_id == 72).astype(F32).astype(BF16)
-    panel_part = jnp.concatenate([in_order(received, g, 0) for g in range(GROUPS)], axis=0)
+    panel_part = jnp.concatenate(firsts, axis=0)
     panel_part = jnp.where(lane >= 112, panel_part, 0.0).astype(BF16)
-    route_part = jnp.concatenate([in_order(received, g, LANES) for g in range(GROUPS)], axis=0)
+    route_part = jnp.concatenate(seconds, axis=0)
     route_part = jnp.where(lane == 72, route_part, 0.0).astype(BF16)
     spread[...] = jnp.dot(panel_part, copy_panel, preferred_element_type=F32)
     target[...] = jnp.dot(route_part, copy_route, preferred_element_type=F32)

time: 61.8 us -> 61.8 us (level)
  no operation moved by 1% of the time
where the time goes in v5:
time: 61.8 us; the launch traced here: 61.5 us
  blocking collectives  37.5 us (61%)
  starting transfers between devices  13.9 us (22%)
  Pallas kernels  8.08 us (13%)
  waiting for transfers between devices  2.01 us (3%)
    all_to_all x1, blocking collectives, body(): lax.all_to_all(joined, 'gy', split_axis=0, concat_axis=0, tiled=True, axi...  19.7 us
    all_to_all x1, starting transfers between devices, body(): lax.all_to_all(packed, 'gx', split_axis=0, concat_axis=0, tiled=True, axi...  13.9 us
    all_to_all x1, blocking collectives, body(): lax.all_to_all(answer, 'gx', split_axis=0, concat_axis=0, tiled=True, axi...  10.8 us
    all_to_all x1, blocking collectives, body(): lax.all_to_all(sent, 'gy', split_axis=0, concat_axis=0, tiled=True, axis_...  6.97 us
    pallas_call x1, Pallas kernels, body(): pl.pallas_call(prepare_x, out_shape=(shape((512, 256), BF16), shape((CX *...  2.87 us
    pallas_call x1, Pallas kernels, body(): pl.pallas_call(prepare_y, out_shape=(shape((8 * 27, 8, LANES), F32), shap...  2.09 us
    all_to_all x1, waiting for transfers between devices, body(): lax.all_to_all(packed, 'gx', split_axis=0, concat_axis=0, tiled=True, axi...  2.01 us
  transfers between devices with their start and end apart: 1, of which 1 were waited for; matrix products, arithmetic and copies ran while one was open for 0% of the time, Pallas kernels for 3%

profile of v5, /device:TPU:1, one launch (start us, length us, event | category | flops | bytes accessed | tf_op | source)
XLA Modules:
  0.0 61.5 jit_solution(2189875754601993806)
XLA Ops:
  0.0 0.0 copy-start.1
  0.0 2.9 %prepare_x.1 = (bf16[512,256]{1,0:T(8,128)(2,1)}, f32[48,4,128]{2,1,0:T(4,128)}) custom-call(f32[3,16,512]{2,1,0:T(8,128)} %bitcast.26, f32[16,2,512]{2,1,0:T(2,128)} %refs_1_.1, bf16[27,16,512]{2,1,0:T(8,128)(2,1)} %bitcast.14, s32[16,512]{1,0:T(8,128)} %refs_3_.1, bf16[4,4,512]{2,1,0:T(4,128)(2,1)} %refs_4_.1, s32[4,4]{1,0:T(4,128)} %refs_5_.1, ...), custom_call_target="tpu_custom_call" | custom-call | tf_op jit(solution)/shard_map/prepare_x/pallas_call | solution.py:454
  2.9 13.9 %all-to-all-start = ((bf16[32,16,256]{2,1,0:T(8,128)(2,1)}), bf16[32,16,256]{2,1,0:T(8,128)(2,1)S(1)}, u32[]{:S(2)}, u32[]{:S(2)}) async-start(bf16[32,16,256]{2,1,0:T(8,128)(2,1)} %bitcast.25), calls=%async_computation | async-start | bytes 524288 | tf_op jit(solution)/shard_map/all_to_all | solution.py:470
  16.8 0.0 copy-done.1
  16.8 2.1 %prepare_y.1 = (f32[216,8,128]{2,1,0:T(8,128)S(1)}, f32[216,128]{1,0:T(8,128)S(1)}, f32[56,128]{1,0:T(8,128)S(1)}, s32[8,128]{1,0:T(8,128)S(1)}) custom-call(s32[1]{0:T(128)} %bitcast.place, bf16[27,16,512]{2,1,0:T(8,128)(2,1)S(1)} %bitcast.23), custom_call_target="tpu_custom_call" | custom-call | tf_op jit(solution)/shard_map/prepare_y/pallas_call | solution.py:471
  18.9 0.0 copy-start
  18.9 2.0 %all-to-all-done = bf16[32,16,256]{2,1,0:T(8,128)(2,1)S(1)} async-done(((bf16[32,16,256]{2,1,0:T(8,128)(2,1)}), bf16[32,16,256]{2,1,0:T(8,128)(2,1)S(1)}, u32[]{:S(2)}, u32[]{:S(2)}) %all-to-all-start) | async-done | bytes 262176 | tf_op jit(solution)/shard_map/all_to_all | solution.py:470
  20.9 1.2 %solve_x.1 = bf16[512,128]{1,0:T(8,128)(2,1)S(1)} custom-call(bf16[512,256]{1,0:T(8,128)(2,1)S(1)} %bitcast.18), custom_call_target="tpu_custom_call" | custom-call | tf_op jit(solution)/shard_map/solve_x/pallas_call | solution.py:486
  22.1 0.0 copy-start.2
  22.1 10.8 %all_to_all.45 = bf16[32,16,128]{2,1,0:T(8,128)(2,1)S(1)} all-to-all(bf16[32,16,128]{2,1,0:T(8,128)(2,1)S(1)} %bitcast.22), channel_id=1, replica_groups={{320,336,352,368,384,400,416,432,448,464,480,496,0,16,32,48,64,80,96,11..., dimensions={0} | all-to-all | bytes 262144 | tf_op jit(solution)/shard_map/all_to_all | solution.py:501
  32.9 0.0 copy-done
  32.9 0.0 copy-done.2
  32.9 0.8 %finish_x.1 = (f32[288,128]{1,0:T(8,128)S(1)}, f32[24,8,128]{2,1,0:T(8,128)S(1)}, f32[48,128]{1,0:T(8,128)S(1)}) custom-call(bf16[512,128]{1,0:T(8,128)(2,1)S(1)} %bitcast.21, f32[48,4,128]{2,1,0:T(4,128)S(1)} %copy-done.2, bf16[27,16,512]{2,1,0:T(8,128)(2,1)S(1)} %bitcast.15, f32[216,8,128]{2,1,0:T(8,128)S(1)} %get-tuple-element.21.turned, ...), custom_call_target="tpu_custom_call" | custom-call | tf_op jit(solution)/shard_map/finish_x/pallas_call | solution.py:502
  33.7 7.0 %all_to_all.46 = f32[4,72,128]{2,1,0:T(8,128)S(1)} all-to-all(f32[4,72,128]{2,1,0:T(8,128)S(1)} %bitcast.24), channel_id=1, replica_groups={{1,2,3,0},{5,6,7,4},{9,10,11,8},{13,14,15,12},{17,18,19,16},{21,22,23,2..., dimensions={0} | all-to-all | bytes 294912 | tf_op jit(solution)/shard_map/all_to_all | solution.py:520
  40.7 0.1 join_y.1
  40.8 19.7 %all_to_all.47 = f32[4,72,128]{2,1,0:T(8,128)S(1)} all-to-all(f32[4,72,128]{2,1,0:T(8,128)S(1)} %bitcast.20), channel_id=1, replica_groups={{8,4,0,12},{9,5,1,13},{10,6,2,14},{11,7,3,15},{24,20,16,28},{25,21,17,2..., dimensions={0} | all-to-all | bytes 294912 | tf_op jit(solution)/shard_map/all_to_all | solution.py:529
  60.5 1.0 %finish_y.1 = f32[3,16,512]{2,1,0:T(8,128)} custom-call(s32[8,128]{1,0:T(8,128)S(1)} %get-tuple-element.16.spot, f32[288,128]{1,0:T(8,128)S(1)} %bitcast.17, f32[288,128]{1,0:T(8,128)S(1)} %bitcast.19, f32[24,8,128]{2,1,0:T(8,128)S(1)} %get-tuple-element.25.values, f32[48,128]{1,0:T(8,128)S(1)} %get-tuple-element.26.ends, ...), custom_call_target="tpu_custom_call" | custom-call | tf_op jit(solution)/shard_map/finish_y/pallas_call | solution.py:530
Async XLA Ops:
  0.0 16.8 %copy-start.1 = (bf16[16,27,512]{2,0,1:T(8,128)(2,1)S(1)}, bf16[16,27,512]{2,0,1:T(8,128)(2,1)}, u32[]{:S(2)}) copy-start(bf16[16,27,512]{2,0,1:T(8,128)(2,1)} %param.11) | copy-start | bytes 1327108
  2.9 18.0 %all-to-all-start = ((bf16[32,16,256]{2,1,0:T(8,128)(2,1)}), bf16[32,16,256]{2,1,0:T(8,128)(2,1)S(1)}, u32[]{:S(2)}, u32[]{:S(2)}) async-start(bf16[32,16,256]{2,1,0:T(8,128)(2,1)} %bitcast.25), calls=%async_computation | async-start | bytes 524288 | tf_op jit(solution)/shard_map/all_to_all | solution.py:470
  18.9 14.0 %copy-start = (bf16[16,27,512]{2,0,1:T(8,128)(2,1)S(1)}, bf16[16,27,512]{2,0,1:T(8,128)(2,1)}, u32[]{:S(2)}) copy-start(bf16[16,27,512]{2,0,1:T(8,128)(2,1)} %param.10) | copy-start | bytes 1327108
  22.1 10.8 %copy-start.2 = (f32[48,4,128]{2,1,0:T(4,128)S(1)}, f32[48,4,128]{2,1,0:T(4,128)}, u32[]{:S(2)}) copy-start(f32[48,4,128]{2,1,0:T(4,128)} %get-tuple-element.20.base) | copy-start | bytes 294916
